TPU v7x, 32 devices: a whole 2x2x4 slice. The times are simulated.
32 devices in a mesh: groups: 2 (over y), row: 4 (over z), col: 2 (over x), freq: 2 (over core).
Axes of the slice: x: 2, y: 2, z: 4, core: 2. Of those that a mesh axis runs over, the one named last changes fastest.
Arguments:
- records: bfloat16 [16, 3072, 5120], P(('groups', 'freq'), ('row', 'col')), parts along dimension 0, may hold values from -1000 to 1000
- live_mask: int32 [10240], P(('groups', 'col')), parts along dimension 0, may hold values 0 or 1
- bin_index: int32 [8], P('groups'), parts along dimension 0, may hold values from 7 to 613
- block_order: int32 [8], P('groups'), parts along dimension 0, may hold values from 0 to 3, each once
Outputs:
- cross_stack: float32 [8, 2, 5120, 5120], P(('groups', 'freq'), None, 'row', 'col'), parts along dimension 0
There are 2 independent parts, one for each index of `groups`. A program takes and returns all parts, laid end to end along the dimension named above; each array names one. Nothing has to cross between parts.
Inputs may be any that keep to these rules, and one draw needn't show every extreme that they name: `bin_index`: bin numbers may repeat. `block_order`: each of the 4 channel blocks once.
All inputs are finite; a program needn't handle non-finite values. No bound on the sum of `live_mask` on one device may be relied on, other than what follows from the above.
Results may differ from a plain program's by a relative error of at most 0.0059.
Values may be sent and summed in bfloat16 or wider, within the bound.
A program may use at most 192 MiB of HBM per device.

v0:
```python
import math

import jax
import jax.numpy as jnp
from jax import lax
from jax.sharding import PartitionSpec as P

C = 5120
S = 3072


def dft_rows(bin_index, positions):
    length = S
    phase_step = bin_index[:, None] * positions[None, :] % length
    angles = 2.0 * math.pi / length * phase_step.astype(jnp.float32)
    window = 0.5 - 0.5 * jnp.cos(2.0 * math.pi / length * positions.astype(jnp.float32))
    factor = math.sqrt(16.0 / (3.0 * length)) * window
    real_part = factor[None, :] * jnp.cos(angles)
    imag_part = -factor[None, :] * jnp.sin(angles)
    return jnp.stack([real_part, imag_part], axis=1).astype(jnp.bfloat16)


def local(records, live_mask, bin_index, block_order):
    half_windows, local_samples, channels = records.shape
    segment = lax.axis_index(("row", "col"))
    positions = segment * local_samples + jnp.arange(local_samples, dtype=jnp.int32)
    dft_table = dft_rows(bin_index, positions).reshape(-1, local_samples)
    spectra = jnp.einsum("ks,wsc->wkc", dft_table, records, preferred_element_type=jnp.float32)
    energy = jnp.sum(jnp.square(records.astype(jnp.float32)), axis=1, keepdims=True)
    block_width = live_mask.shape[0]
    spectra, energy = lax.psum((spectra, energy), ("row", "col"))
    offset = lax.axis_index("col") * block_width
    spectra = lax.dynamic_slice_in_dim(spectra, offset, block_width, 2)
    energy = lax.dynamic_slice_in_dim(energy, offset, block_width, 2)
    part_width = live_mask.shape[0]
    scaling = live_mask.astype(jnp.float32)[None, None, :] / jnp.sqrt(energy / S + 1e-06)
    total_bins = spectra.shape[1] // 2
    coeffs = (
        (spectra * scaling).astype(jnp.bfloat16).reshape(half_windows, total_bins, 2, part_width)
    )
    columns = lax.all_to_all(coeffs, "freq", split_axis=1, concat_axis=0, tiled=True)
    windows = columns.shape[0]
    row_width = C // lax.axis_size("row")
    per_block = block_width // row_width
    chosen = block_order[lax.axis_index("row")]
    own_slice = lax.dynamic_slice_in_dim(columns, chosen % per_block * row_width, row_width, 3)
    gathered = lax.all_gather(own_slice, "col", axis=3, tiled=True)
    sources = lax.dynamic_slice_in_dim(gathered, chosen // per_block * row_width, row_width, 3)
    turned = jnp.stack([sources[:, :, 1], -sources[:, :, 0]], axis=2)
    paired = jnp.stack([sources, turned], axis=1)
    products = jnp.einsum("wpbti,wbtj->bpij", paired, columns, preferred_element_type=jnp.float32)
    return products / windows


def solution(mesh):
    return jax.shard_map(
        local,
        mesh=mesh,
        in_specs=(
            P(("groups", "freq"), ("row", "col"), None),
            P(("groups", "col")),
            P("groups"),
            P("groups"),
        ),
        out_specs=P(("groups", "freq"), None, "row", "col"),
        check_vma=False,
    )
```

profile of v0, /device:TPU:0, one launch (start us, length us, event | category | flops | bytes accessed | tf_op | source)
XLA Modules:
  0.0 140.2 jit_solution(2948241069834562225)
XLA Ops:
  6.5 0.0 copy-start.1
  6.5 0.0 copy-start
  6.5 0.0 all-reduce.3.cloned.1.call-start
  6.5 0.1 subtract_multiply_fusion
  6.6 0.8 multiply_convert_fusion.2
  7.4 7.5 %multiply_reduce_fusion = f32[4,5120]{1,0:T(4,128)} fusion(bf16[4,384,5120]{2,1,0:T(8,128)(2,1)} %param.4), kind=kLoop, calls=%fused_computation.1 | loop fusion | flops 23572480 | bytes 15810560 | tf_op jit(solution)/shard_map/reduce_sum | solution.py:29
  14.9 8.4 %convolution_bitcast_fusion = f32[4,8,5120]{2,1,0:T(8,128)} fusion(bf16[8,384,1]{1,0,2:T(8,128)(2,1)S(1)} %reshape.171, bf16[4,384,5120]{2,1,0:T(8,128)(2,1)} %param.4), kind=kOutput, calls=%fused_computation.2 | convolution fusion | flops 125829120 | bytes 16390144 | tf_op jit(solution)/shard_map/ks,wsc->wkc/dot_general | solution.py:28
  23.4 0.0 all-reduce.3.cloned.1.call-update
  23.4 0.0 copy-done.1
  23.4 0.7 dynamic_slice.17
  26.8 0.0 copy-done
  26.8 73.8 %all-reduce.3.cloned.1.call-done = (f32[4,8,5120]{2,1,0:T(8,128)}, f32[4,1,5120]{2,0,1:T(4,128)}) async-done(((f32[4,8,5120]{2,1,0:T(8,128)}, f32[4,1,5120]{2,0,1:T(4,128)}), (f32[4,8,5120]{2,1,0:T(8,128)}, f32[4,1,5120]{2,0,1:T(4,128)})) %all-reduce.3.cloned.1.call-update) | async-done | bytes 737296 | tf_op jit(solution)/shard_map/psum | solution.py:31
  100.6 0.8 multiply_bitcast_fusion
  101.4 1.0 multiply_convert_fusion
  102.4 0.1 reshape.170
  102.5 0.1 copy.14
  102.6 3.8 %all_to_all.18 = bf16[4,4,2,2560]{3,2,0,1:T(2,128)(2,1)S(1)} all-to-all(bf16[4,4,2,2560]{3,2,0,1:T(2,128)(2,1)S(1)} %copy.14), channel_id=1, replica_groups=mesh['groups'=2,'row'=4,'col'=2,'freq'=2] {'freq'}, dimensions={1} | all-to-all | bytes 327680 | tf_op jit(solution)/shard_map/all_to_all | solution.py:41
  106.5 0.1 copy.22
  106.6 5.2 %all_gather.3 = bf16[8,2,2,2560]{3,0,2,1:T(8,128)(2,1)S(1)} all-gather(bf16[8,2,2,1280]{3,0,2,1:T(8,128)(2,1)S(1)} %constant_dynamic-slice_fusion.1), channel_id=1, replica_groups=mesh['groups'=2,'row'=4,'col'=2,'freq'=2] {'col'}, dimensions={3}, use_global_device_ids=true | all-gather | bytes 245760 | tf_op jit(solution)/shard_map/all_gather | solution.py:47
  111.9 21.5 %bitcast_multiply_fusion = f32[2,2,1280,2560]{3,2,1,0:T(8,128)} fusion(bf16[8,2,2,2560,1]{3,0,2,1,4:T(8,128)(2,1)S(1)} %reshape.172, bf16[8,1,2,2,1280]{4,0,3,2,1:T(8,128)(2,1)S(1)} %maximum_bitcast_fusion, bf16[8,1,2,2,1280]{4,0,3,2,1:T(8,128)(2,1)S(1)} %dynamic-slice_bitcast_fusion), kind=kOutput, calls=%fused_computation | convolution fusion | flops 432619520 | bytes 52756480 | tf_op jit(solution)/shard_map/wpbti,wbtj->bpij/dot_general | solution.py:51
  (11 shorter events, 0.2 us)
Async XLA Ops:
  6.5 16.9 %copy-start.1 = (s32[4]{0:T(128)S(1)}, s32[4]{0:T(128)}, u32[]{:S(2)}) copy-start(s32[4]{0:T(128)} %param.7) | copy-start | bytes 52
  6.5 20.2 %copy-start = (s32[2560]{0:T(1024)S(1)}, s32[2560]{0:T(1024)}, u32[]{:S(2)}) copy-start(s32[2560]{0:T(1024)} %param.5) | copy-start | bytes 30724
  6.5 94.1 %all-reduce.3.cloned.1.call-start = ((), (), s32[]{:S(2)}) async-start(), calls=%async_computation.1 | async-start | bytes 1474560 | tf_op jit(solution)/shard_map/psum | solution.py:31
Sparse Core Ops, SparseCore 0:
  23.5 77.0 all-reduce.2
where the time goes:
time: 141 us; the launch traced here: 140 us
  waiting for transfers between devices  73.8 us (52%)
  matrix products  30 us (21%)
  between operations  16.2 us (11%)
  other arithmetic  10.2 us (7%)
  blocking collectives  9.03 us (6%)
    psum x1, waiting for transfers between devices, local(): spectra, energy = lax.psum((spectra, energy), ('row', 'col'))  73.8 us
    dot_general x1, matrix products, local(): jnp.einsum('wpbti,wbtj->bpij', paired, columns, preferred_element_type=jn...  21.5 us
    dot_general x1, matrix products, local(): jnp.einsum('ks,wsc->wkc', dft_table, records, preferred_element_type=jnp....  8.45 us
    reduce_sum x1, other arithmetic, local(): jnp.sum(jnp.square(records.astype(jnp.float32)), axis=1, keepdims=True)  7.46 us
    all_gather x1, blocking collectives, local(): gathered = lax.all_gather(own_slice, 'col', axis=3, tiled=True)  5.18 us
    all_to_all x1, blocking collectives, local(): lax.all_to_all(coeffs, 'freq', split_axis=1, concat_axis=0, tiled=True)  3.85 us
  transfers between devices with their start and end apart: 1, of which 1 were waited for; matrix products, arithmetic and copies ran while one was open for 0% of the time, Pallas kernels for 0%

commit v1 on v0

--- a/solution.py
+++ b/solution.py
@@ -1,12 +1,18 @@
+import functools
 import math
 
 import jax
 import jax.numpy as jnp
 from jax import lax
+from jax.experimental import pallas as pl
+from jax.experimental.pallas import tpu as pltpu
 from jax.sharding import PartitionSpec as P
 
 C = 5120
 S = 3072
+AHEAD = 3
+TILE_ROWS = 256
+MESH = pl.DeviceIdType.MESH
 
 
 def dft_rows(bin_index, positions):
@@ -20,7 +26,7 @@
     return jnp.stack([real_part, imag_part], axis=1).astype(jnp.bfloat16)
 
 
-def local(records, live_mask, bin_index, block_order):
+def plain(records, live_mask, bin_index, block_order):
     half_windows, local_samples, channels = records.shape
     segment = lax.axis_index(("row", "col"))
     positions = segment * local_samples + jnp.arange(local_samples, dtype=jnp.int32)
@@ -52,9 +58,276 @@
     return products / windows
 
 
+def coeffs_kernel(
+    rows, width, table_ref, mask_ref, records_ref, out_ref,
+    rec, part, xs, xr, zs, zr, ag,
+    rec_sem, xs_sem, xr_sem, zs_sem, zr_sem, own_sem, gs_sem, gr_sem, fs_sem, fr_sem,
+):
+    r, c, f = lax.axis_index("row"), lax.axis_index("col"), lax.axis_index("freq")
+    windows, samples = records_ref.shape[0], records_ref.shape[1]
+    steps = 2 * rows
+
+    def peer(step):
+        return lax.rem(r + 1 + step, rows)
+
+    def load(step):
+        col = lax.rem(c + 1 + lax.div(step, rows), 2)
+        start = pl.multiple_of((col * rows + peer(step)) * width, 128)
+        return pltpu.make_async_copy(
+            records_ref.at[:, :, pl.ds(start, width)], rec.at[step], rec_sem.at[step]
+        )
+
+    def x_copy(step):
+        return pltpu.make_async_remote_copy(
+            src_ref=xs.at[step], dst_ref=xr.at[step],
+            send_sem=xs_sem.at[step], recv_sem=xr_sem.at[step],
+            device_id={"col": 1 - c}, device_id_type=MESH,
+        )
+
+    def z_copy(step):
+        return pltpu.make_async_remote_copy(
+            src_ref=zs.at[step], dst_ref=zr.at[step],
+            send_sem=zs_sem.at[step], recv_sem=zr_sem.at[step],
+            device_id={"row": peer(step)}, device_id_type=MESH,
+        )
+
+    def piece(col, row, half):
+        return out_ref.at[
+            col,
+            pl.ds(pl.multiple_of(half * 16, 16), 16),
+            pl.ds(pl.multiple_of(row * width, 128), width),
+        ]
+
+    def compute(step):
+        load(step).wait()
+        for w in range(windows):
+            part[8 * w : 8 * w + 8, :] = jnp.dot(
+                table_ref[...], rec[step, w], preferred_element_type=jnp.float32
+            )
+            total = jnp.zeros((8, width), jnp.float32)
+            for s in range(0, samples, 16):
+                x = rec[step, w, s : s + 16, :].astype(jnp.float32)
+                x = x * x
+                total = total + (x[:8] + x[8:])
+            part[32 + w : 33 + w, :] = jnp.sum(total, axis=0, keepdims=True)
+
+    barrier = pltpu.get_barrier_semaphore()
+    for step in range(rows - 1):
+        for half in range(2):
+            pl.semaphore_signal(
+                barrier, inc=1, device_id={"row": peer(step), "freq": half}, device_id_type=MESH
+            )
+    pl.semaphore_signal(barrier, inc=1, device_id={"freq": 1 - f}, device_id_type=MESH)
+    pl.semaphore_signal(barrier, inc=1, device_id={"col": 1 - c}, device_id_type=MESH)
+
+    for step in range(AHEAD):
+        load(step).start()
+    part[...] = jnp.zeros_like(part)
+    pl.semaphore_wait(barrier, 2 * rows)
+
+    @pl.loop(0, rows)
+    def _(step):
+        load(step + AHEAD).start()
+        compute(step)
+        xs[step] = part[...].astype(xs.dtype)
+        x_copy(step).start()
+
+    @pl.loop(0, rows - 1)
+    def _(step):
+        @pl.when(step + rows + AHEAD < steps)
+        def _():
+            load(step + rows + AHEAD).start()
+
+        compute(step + rows)
+        x_copy(step).wait_recv()
+        both = part[...] + xr[step].astype(jnp.float32)
+        zs[step] = both[:40].astype(zs.dtype)
+        z_copy(step).start()
+
+    compute(steps - 1)
+    x_copy(rows - 1).wait_recv()
+    total = (part[...] + xr[rows - 1].astype(jnp.float32))[:40]
+    for step in range(rows - 1):
+        z_copy(step).wait_recv()
+        total = total + zr[step].astype(jnp.float32)
+
+    mask = mask_ref[:, pl.ds(pl.multiple_of(r * width, 128), width)].astype(jnp.float32)
+    scaling = mask / jnp.sqrt(total[32:36] / S + 1e-06)
+    coeffs = jnp.concatenate(
+        [total[8 * w : 8 * w + 8] * scaling[w : w + 1] for w in range(windows)], axis=0
+    ).astype(jnp.bfloat16)
+    to = lax.broadcasted_iota(jnp.int32, (16, 32), 0)
+    of = lax.broadcasted_iota(jnp.int32, (16, 32), 1)
+    for half in range(2):
+        pick = (of == (to // 4) * 8 + 4 * half + to % 4).astype(jnp.float32).astype(jnp.bfloat16)
+        ag[half] = jnp.dot(pick, coeffs, preferred_element_type=jnp.float32).astype(jnp.bfloat16)
+
+    def gather_copy(step, half, src_half):
+        return pltpu.make_async_remote_copy(
+            src_ref=ag.at[half], dst_ref=piece(c, r, f),
+            send_sem=gs_sem.at[step, half], recv_sem=gr_sem.at[step, f],
+            device_id={"row": peer(step), "freq": half}, device_id_type=MESH,
+        )
+
+    def arrival(step, half):
+        row = lax.rem(r + rows - 1 - step, rows)
+        return pltpu.make_async_remote_copy(
+            src_ref=ag.at[0], dst_ref=piece(c, row, half),
+            send_sem=gs_sem.at[step, half], recv_sem=gr_sem.at[step, half],
+            device_id={"row": peer(step), "freq": half}, device_id_type=MESH,
+        )
+
+    def forward(step, half, src):
+        row = lax.rem(r + rows - 1 - step, rows)
+        return pltpu.make_async_remote_copy(
+            src_ref=src, dst_ref=piece(c, row, half),
+            send_sem=fs_sem.at[step, half], recv_sem=fr_sem.at[step, half],
+            device_id={"col": 1 - c}, device_id_type=MESH,
+        )
+
+    def forwarded(step, half):
+        row = lax.rem(r + rows - 1 - step, rows)
+        return pltpu.make_async_remote_copy(
+            src_ref=ag.at[0], dst_ref=piece(1 - c, row, half),
+            send_sem=fs_sem.at[step, half], recv_sem=fr_sem.at[step, half],
+            device_id={"col": 1 - c}, device_id_type=MESH,
+        )
+
+    last = rows - 1
+    own = pltpu.make_async_copy(ag.at[f], piece(c, r, f), own_sem)
+    own.start()
+    to_core = pltpu.make_async_remote_copy(
+        src_ref=ag.at[1 - f], dst_ref=piece(c, r, f),
+        send_sem=gs_sem.at[last, 1 - f], recv_sem=gr_sem.at[last, f],
+        device_id={"freq": 1 - f}, device_id_type=MESH,
+    )
+    for step in range(rows - 1):
+        for half in range(2):
+            gather_copy(step, half, half).start()
+    to_core.start()
+    forward(last, f, ag.at[f]).start()
+    from_core = pltpu.make_async_remote_copy(
+        src_ref=ag.at[0], dst_ref=piece(c, r, 1 - f),
+        send_sem=gs_sem.at[last, f], recv_sem=gr_sem.at[last, 1 - f],
+        device_id={"freq": 1 - f}, device_id_type=MESH,
+    )
+    from_core.wait_recv()
+    forward(last, 1 - f, piece(c, r, 1 - f)).start()
+    for step in range(rows - 1):
+        for half in range(2):
+            arrival(step, half).wait_recv()
+            row = lax.rem(r + rows - 1 - step, rows)
+            forward(step, half, piece(c, row, half)).start()
+
+    for step in range(rows):
+        for half in range(2):
+            forwarded(step, half).wait_recv()
+    own.wait()
+    to_core.wait_send()
+    for step in range(rows):
+        x_copy(step).wait_send()
+        for half in range(2):
+            forwarded(step, half).wait_send()
+    for step in range(rows - 1):
+        z_copy(step).wait_send()
+        for half in range(2):
+            gather_copy(step, half, half).wait_send()
+
+
+def products_kernel(row_width, scale, order_ref, coeffs_ref, out_ref):
+    variant, tile = pl.program_id(0), pl.program_id(1)
+    chosen = order_ref[lax.axis_index("row")]
+    per_block = coeffs_ref.shape[2] // row_width
+    tile_rows = out_ref.shape[2]
+    start = pl.multiple_of(lax.rem(chosen, per_block) * row_width + tile * tile_rows, 128)
+    sources = coeffs_ref[lax.div(chosen, per_block), :, pl.ds(start, tile_rows)]
+    depth = sources.shape[0]
+    of = lax.broadcasted_iota(jnp.int32, (depth, depth), 0)
+    to = lax.broadcasted_iota(jnp.int32, (depth, depth), 1)
+    imag = lax.rem(variant, 2)
+    odd = to & 1
+    same_bin = ((to >> 1) & 1) == lax.div(variant, 2)
+    partner = to + imag * (1 - 2 * odd)
+    sign = (1 - 2 * odd * imag).astype(jnp.float32)
+    pick = jnp.where(same_bin & (of == partner), sign, 0.0).astype(jnp.bfloat16)
+    paired = lax.dot_general(
+        sources, pick, (((0,), (0,)), ((), ())), preferred_element_type=jnp.float32
+    ).astype(jnp.bfloat16)
+    columns = coeffs_ref[lax.axis_index("col")]
+    out_ref[0, 0] = jnp.dot(paired, columns, preferred_element_type=jnp.float32) * scale
+
+
+def local(records, live_mask, bin_index, block_order):
+    half_windows, local_samples, channels = records.shape
+    rows = lax.axis_size("row")
+    block_width = live_mask.shape[0]
+    width = block_width // rows
+    row_width = C // rows
+    segment = lax.axis_index(("row", "col"))
+    positions = segment * local_samples + jnp.arange(local_samples, dtype=jnp.int32)
+    table = dft_rows(bin_index, positions).reshape(-1, local_samples)
+    vmem = pl.BlockSpec(memory_space=pltpu.VMEM)
+    anywhere = pl.BlockSpec(memory_space=pl.ANY)
+    dma = pltpu.SemaphoreType.DMA
+    coeffs = pl.pallas_call(
+        functools.partial(coeffs_kernel, rows, width),
+        out_shape=jax.ShapeDtypeStruct((2, 32, block_width), jnp.bfloat16),
+        in_specs=[vmem, vmem, anywhere],
+        out_specs=anywhere,
+        scratch_shapes=[
+            pltpu.VMEM((2 * rows, half_windows, local_samples, width), jnp.bfloat16),
+            pltpu.VMEM((48, width), jnp.float32),
+            pltpu.VMEM((rows, 48, width), jnp.bfloat16),
+            pltpu.VMEM((rows, 48, width), jnp.bfloat16),
+            pltpu.VMEM((rows - 1, 40, width), jnp.float32),
+            pltpu.VMEM((rows - 1, 40, width), jnp.float32),
+            pltpu.VMEM((2, 16, width), jnp.bfloat16),
+            dma((2 * rows,)),
+            dma((rows,)),
+            dma((rows,)),
+            dma((rows - 1,)),
+            dma((rows - 1,)),
+            dma(()),
+            dma((rows, 2)),
+            dma((rows, 2)),
+            dma((rows, 2)),
+            dma((rows, 2)),
+        ],
+        compiler_params=pltpu.CompilerParams(
+            collective_id=0, has_side_effects=True, vmem_limit_bytes=40 * 1024 * 1024
+        ),
+        cost_estimate=pl.CostEstimate(
+            flops=18 * records.size, bytes_accessed=2 * records.size, transcendentals=0
+        ),
+        name="window_coeffs",
+    )(table, live_mask.reshape(1, -1), records)
+    out_shape = (2, 2, row_width, block_width)
+    return pl.pallas_call(
+        functools.partial(products_kernel, row_width, 1.0 / (2 * half_windows)),
+        out_shape=jax.ShapeDtypeStruct(out_shape, jnp.float32),
+        grid_spec=pltpu.PrefetchScalarGridSpec(
+            num_scalar_prefetch=1,
+            grid=(4, row_width // TILE_ROWS),
+            in_specs=[pl.BlockSpec((2, 32, block_width), lambda v, i, order: (0, 0, 0))],
+            out_specs=pl.BlockSpec(
+                (1, 1, TILE_ROWS, block_width), lambda v, i, order: (v // 2, v % 2, i, 0)
+            ),
+        ),
+        compiler_params=pltpu.CompilerParams(vmem_limit_bytes=32 * 1024 * 1024),
+        cost_estimate=pl.CostEstimate(
+            flops=64 * math.prod(out_shape),
+            bytes_accessed=4 * math.prod(out_shape),
+            transcendentals=0,
+        ),
+        name="cross_products",
+    )(block_order, coeffs)
+
+
 def solution(mesh):
+    rows, cols = mesh.shape["row"], mesh.shape["col"]
+    small = cols == 2 and mesh.shape["freq"] == 2 and rows == 4
     return jax.shard_map(
-        local,
+        local if small else plain,
         mesh=mesh,
         in_specs=(
             P(("groups", "freq"), ("row", "col"), None),

time: 141 us -> 54.6 us (0.39)
  waiting for transfers between devices: 73.8 us -> 0 us
  Pallas kernels: 0 us -> 52.1 us
  matrix products: 30 us -> 0 us
  between operations: 16.2 us -> 0.04 us
  other arithmetic: 10.2 us -> 0.86 us
  blocking collectives: 9.03 us -> 0 us
    psum x1 -> x0, waiting for transfers between devices: 73.8 us -> none  [local(): spectra, energy = lax.psum((spectra, energy), ('row', 'col'))]
    pallas_call x0 -> x2, Pallas kernels: none -> 52.1 us  [the longest x1 29.2 us: local(): pl.pallas_call(functools.partial(coeffs_kernel, rows, width), out_shape=j...]
    dot_general x2 -> x0, matrix products: 30 us -> none  [the longest x1 21.5 us: local(): jnp.einsum('wpbti,wbtj->bpij', paired, columns, preferred_element_type=jn...]
    reduce_sum x1 -> x0, other arithmetic: 7.46 us -> none  [local(): jnp.sum(jnp.square(records.astype(jnp.float32)), axis=1, keepdims=True)]
    all_gather x1 -> x0, blocking collectives: 5.18 us -> none  [local(): gathered = lax.all_gather(own_slice, 'col', axis=3, tiled=True)]
    all_to_all x1 -> x0, blocking collectives: 3.85 us -> none  [local(): lax.all_to_all(coeffs, 'freq', split_axis=1, concat_axis=0, tiled=True)]
  transfers between devices with their start and end apart: 1 -> 0, of which waited for: 1 -> 0; matrix products, arithmetic and copies ran while one was open for 0% -> 0% of each run, Pallas kernels for 0% -> 0%
where the time goes in v1:
time: 54.6 us; the launch traced here: 54.4 us
  Pallas kernels  52.1 us (95%)
  local copies, waits for them, and re-layouts  1.39 us (3%)
  other arithmetic  0.86 us (2%)
    pallas_call x1, Pallas kernels, local(): pl.pallas_call(functools.partial(coeffs_kernel, rows, width), out_shape=j...  29.2 us
    pallas_call x1, Pallas kernels, local(): pl.pallas_call(functools.partial(products_kernel, row_width, 1.0 / (2 * h...  22.9 us

profile of v1, /device:TPU:0, one launch (start us, length us, event | category | flops | bytes accessed | tf_op | source)
XLA Modules:
  0.0 54.4 jit_solution(18250901080319335628)
XLA Ops:
  0.1 0.8 %multiply_convert_fusion.1 = (bf16[4,1,384]{2,0,1:T(4,128)(2,1)S(1)}, bf16[4,1,384]{2,0,1:T(4,128)(2,1)S(1)}) fusion(s32[384]{0:T(512)S(1)} %iota_add_fusion, s32[4]{0:T(128)} %param.6, f32[384]{0:T(512)S(1)} %get-tuple-element.7, f32[384]{0:T(512)S(1)} %get-tuple-element.8), kind=kLoop, calls=%fused_computation.5 | loop fusion | flops 19968 | bytes 10768 | tf_op jit(solution)/shard_map/convert
  0.9 0.7 %reshape.167.mask_ref = s32[1,2560]{1,0:T(1,128)S(1)} reshape(s32[2560]{0:T(1024)} %param.5) | data formatting | bytes 20480 | tf_op jit(solution)/shard_map/reshape | solution.py:303
  1.6 29.2 %window_coeffs.1.coeffs_ref = bf16[2,32,2560]{2,1,0:T(8,128)(2,1)S(1)} custom-call(bf16[8,384]{1,0:T(8,128)(2,1)S(1)} %convert_element_type.31.table_ref, s32[1,2560]{1,0:T(1,128)S(1)} %reshape.167.mask_ref, bf16[4,384,5120]{2,1,0:T(8,128)(2,1)} %records_ref.1), custom_call_target="tpu_custom_call" | custom-call | flops 141557760 | bytes 15728640 | tf_op jit(solution)/shard_map/window_coeffs/pallas_call | solution.py:272
  30.8 0.0 copy-start
  30.8 0.6 %copy-done = s32[4]{0:T(128)S(1)} copy-done((s32[4]{0:T(128)S(1)}, s32[4]{0:T(128)}, u32[]{:S(2)}) %copy-start) | copy-done | bytes 40
  31.5 22.9 %cross_products.1 = f32[2,2,1280,2560]{3,2,1,0:T(8,128)} custom-call(s32[4]{0:T(128)S(1)} %copy-done, bf16[2,32,2560]{2,1,0:T(8,128)(2,1)S(1)} %window_coeffs.1.coeffs_ref), custom_call_target="tpu_custom_call" | custom-call | flops 838860800 | bytes 52428800 | tf_op jit(solution)/shard_map/cross_products/pallas_call | solution.py:305
  (5 shorter events, 0.1 us)
Async XLA Ops:
  30.8 0.7 %copy-start = (s32[4]{0:T(128)S(1)}, s32[4]{0:T(128)}, u32[]{:S(2)}) copy-start(s32[4]{0:T(128)} %order_ref.1) | copy-start | bytes 52

commit v2 on v1

--- a/solution.py
+++ b/solution.py
@@ -12,6 +12,7 @@
 S = 3072
 AHEAD = 3
 TILE_ROWS = 256
+SLOTS = 4
 MESH = pl.DeviceIdType.MESH
 
 
@@ -58,9 +59,20 @@
     return products / windows
 
 
+def cosine(step):
+    half, quarter = S // 2, S // 4
+    fold = jnp.abs(step - half)
+    angle = (2.0 * math.pi / S) * jnp.minimum(fold, half - fold).astype(jnp.float32)
+    z = angle * angle
+    value = jnp.full_like(z, 1.0 / math.factorial(16))
+    for n in range(14, -1, -2):
+        value = (-1.0) ** (n // 2) / math.factorial(n) + z * value
+    return jnp.where(fold > quarter, value, -value)
+
+
 def coeffs_kernel(
-    rows, width, table_ref, mask_ref, records_ref, out_ref,
-    rec, part, xs, xr, zs, zr, ag,
+    rows, width, bins_ref, mask_ref, records_ref, out_ref,
+    rec, table, part, xs, xr, zs, zr, ag,
     rec_sem, xs_sem, xr_sem, zs_sem, zr_sem, own_sem, gs_sem, gr_sem, fs_sem, fr_sem,
 ):
     r, c, f = lax.axis_index("row"), lax.axis_index("col"), lax.axis_index("freq")
@@ -102,7 +114,7 @@
         load(step).wait()
         for w in range(windows):
             part[8 * w : 8 * w + 8, :] = jnp.dot(
-                table_ref[...], rec[step, w], preferred_element_type=jnp.float32
+                table[...], rec[step, w], preferred_element_type=jnp.float32
             )
             total = jnp.zeros((8, width), jnp.float32)
             for s in range(0, samples, 16):
@@ -123,6 +135,14 @@
     for step in range(AHEAD):
         load(step).start()
     part[...] = jnp.zeros_like(part)
+    row = lax.broadcasted_iota(jnp.int32, (8, samples), 0)
+    position = (r * 2 + c) * samples + lax.broadcasted_iota(jnp.int32, (8, samples), 1)
+    bins = jnp.zeros_like(row)
+    for k in range(bins_ref.shape[0]):
+        bins = jnp.where((row >> 1) == k, bins_ref[k], bins)
+    phase = lax.rem(bins * position + (row & 1) * (S // 4), S)
+    taper = math.sqrt(16.0 / (3.0 * S)) * (0.5 - 0.5 * cosine(position))
+    table[...] = (taper * cosine(phase)).astype(table.dtype)
     pl.semaphore_wait(barrier, 2 * rows)
 
     @pl.loop(0, rows)
@@ -141,7 +161,7 @@
         compute(step + rows)
         x_copy(step).wait_recv()
         both = part[...] + xr[step].astype(jnp.float32)
-        zs[step] = both[:40].astype(zs.dtype)
+        zs[step] = both.astype(zs.dtype)
         z_copy(step).start()
 
     compute(steps - 1)
@@ -149,9 +169,9 @@
     total = (part[...] + xr[rows - 1].astype(jnp.float32))[:40]
     for step in range(rows - 1):
         z_copy(step).wait_recv()
-        total = total + zr[step].astype(jnp.float32)
-
-    mask = mask_ref[:, pl.ds(pl.multiple_of(r * width, 128), width)].astype(jnp.float32)
+        total = total + zr[step].astype(jnp.float32)[:40]
+
+    mask = mask_ref[pl.ds(pl.multiple_of(r * width, 128), width)].astype(jnp.float32)[None, :]
     scaling = mask / jnp.sqrt(total[32:36] / S + 1e-06)
     coeffs = jnp.concatenate(
         [total[8 * w : 8 * w + 8] * scaling[w : w + 1] for w in range(windows)], axis=0
@@ -234,27 +254,53 @@
             gather_copy(step, half, half).wait_send()
 
 
-def products_kernel(row_width, scale, order_ref, coeffs_ref, out_ref):
-    variant, tile = pl.program_id(0), pl.program_id(1)
+def products_kernel(row_width, scale, order_ref, coeffs_ref, out_ref, ring, sem):
+    slots, tile_rows = ring.shape[:2]
+    tiles = row_width // tile_rows
+    steps = 4 * tiles
     chosen = order_ref[lax.axis_index("row")]
     per_block = coeffs_ref.shape[2] // row_width
-    tile_rows = out_ref.shape[2]
-    start = pl.multiple_of(lax.rem(chosen, per_block) * row_width + tile * tile_rows, 128)
-    sources = coeffs_ref[lax.div(chosen, per_block), :, pl.ds(start, tile_rows)]
-    depth = sources.shape[0]
-    of = lax.broadcasted_iota(jnp.int32, (depth, depth), 0)
-    to = lax.broadcasted_iota(jnp.int32, (depth, depth), 1)
-    imag = lax.rem(variant, 2)
-    odd = to & 1
-    same_bin = ((to >> 1) & 1) == lax.div(variant, 2)
-    partner = to + imag * (1 - 2 * odd)
-    sign = (1 - 2 * odd * imag).astype(jnp.float32)
-    pick = jnp.where(same_bin & (of == partner), sign, 0.0).astype(jnp.bfloat16)
-    paired = lax.dot_general(
-        sources, pick, (((0,), (0,)), ((), ())), preferred_element_type=jnp.float32
-    ).astype(jnp.bfloat16)
-    columns = coeffs_ref[lax.axis_index("col")]
-    out_ref[0, 0] = jnp.dot(paired, columns, preferred_element_type=jnp.float32) * scale
+    first = lax.rem(chosen, per_block) * row_width
+
+    def store(step):
+        variant = lax.div(step, tiles)
+        start = pl.multiple_of(lax.rem(step, tiles) * tile_rows, tile_rows)
+        slot = lax.rem(step, slots)
+        return pltpu.make_async_copy(
+            ring.at[slot],
+            out_ref.at[lax.div(variant, 2), lax.rem(variant, 2), pl.ds(start, tile_rows)],
+            sem.at[slot],
+        )
+
+    @pl.loop(0, steps)
+    def _(step):
+        @pl.when(step >= slots)
+        def _():
+            store(step - slots).wait()
+
+        variant = lax.div(step, tiles)
+        start = pl.multiple_of(first + lax.rem(step, tiles) * tile_rows, 128)
+        sources = coeffs_ref[lax.div(chosen, per_block), :, pl.ds(start, tile_rows)]
+        depth = sources.shape[0]
+        of = lax.broadcasted_iota(jnp.int32, (depth, depth), 0)
+        to = lax.broadcasted_iota(jnp.int32, (depth, depth), 1)
+        imag = lax.rem(variant, 2)
+        odd = to & 1
+        same_bin = ((to >> 1) & 1) == lax.div(variant, 2)
+        partner = to + imag * (1 - 2 * odd)
+        sign = (1 - 2 * odd * imag).astype(jnp.float32)
+        pick = jnp.where(same_bin & (of == partner), sign, 0.0).astype(jnp.bfloat16)
+        paired = lax.dot_general(
+            sources, pick, (((0,), (0,)), ((), ())), preferred_element_type=jnp.float32
+        ).astype(jnp.bfloat16)
+        columns = coeffs_ref[lax.axis_index("col")]
+        ring[lax.rem(step, slots)] = (
+            jnp.dot(paired, columns, preferred_element_type=jnp.float32) * scale
+        )
+        store(step).start()
+
+    for step in range(steps - slots, steps):
+        store(step).wait()
 
 
 def local(records, live_mask, bin_index, block_order):
@@ -263,24 +309,23 @@
     block_width = live_mask.shape[0]
     width = block_width // rows
     row_width = C // rows
-    segment = lax.axis_index(("row", "col"))
-    positions = segment * local_samples + jnp.arange(local_samples, dtype=jnp.int32)
-    table = dft_rows(bin_index, positions).reshape(-1, local_samples)
+    smem = pl.BlockSpec(memory_space=pltpu.SMEM)
     vmem = pl.BlockSpec(memory_space=pltpu.VMEM)
     anywhere = pl.BlockSpec(memory_space=pl.ANY)
     dma = pltpu.SemaphoreType.DMA
     coeffs = pl.pallas_call(
         functools.partial(coeffs_kernel, rows, width),
         out_shape=jax.ShapeDtypeStruct((2, 32, block_width), jnp.bfloat16),
-        in_specs=[vmem, vmem, anywhere],
+        in_specs=[smem, vmem, anywhere],
         out_specs=anywhere,
         scratch_shapes=[
             pltpu.VMEM((2 * rows, half_windows, local_samples, width), jnp.bfloat16),
+            pltpu.VMEM((8, local_samples), jnp.bfloat16),
             pltpu.VMEM((48, width), jnp.float32),
             pltpu.VMEM((rows, 48, width), jnp.bfloat16),
             pltpu.VMEM((rows, 48, width), jnp.bfloat16),
-            pltpu.VMEM((rows - 1, 40, width), jnp.float32),
-            pltpu.VMEM((rows - 1, 40, width), jnp.float32),
+            pltpu.VMEM((rows - 1, 48, width), jnp.bfloat16),
+            pltpu.VMEM((rows - 1, 48, width), jnp.bfloat16),
             pltpu.VMEM((2, 16, width), jnp.bfloat16),
             dma((2 * rows,)),
             dma((rows,)),
@@ -300,19 +345,17 @@
             flops=18 * records.size, bytes_accessed=2 * records.size, transcendentals=0
         ),
         name="window_coeffs",
-    )(table, live_mask.reshape(1, -1), records)
+    )(bin_index, live_mask, records)
     out_shape = (2, 2, row_width, block_width)
     return pl.pallas_call(
         functools.partial(products_kernel, row_width, 1.0 / (2 * half_windows)),
         out_shape=jax.ShapeDtypeStruct(out_shape, jnp.float32),
-        grid_spec=pltpu.PrefetchScalarGridSpec(
-            num_scalar_prefetch=1,
-            grid=(4, row_width // TILE_ROWS),
-            in_specs=[pl.BlockSpec((2, 32, block_width), lambda v, i, order: (0, 0, 0))],
-            out_specs=pl.BlockSpec(
-                (1, 1, TILE_ROWS, block_width), lambda v, i, order: (v // 2, v % 2, i, 0)
-            ),
-        ),
+        in_specs=[smem, vmem],
+        out_specs=anywhere,
+        scratch_shapes=[
+            pltpu.VMEM((SLOTS, TILE_ROWS, block_width), jnp.float32),
+            dma((SLOTS,)),
+        ],
         compiler_params=pltpu.CompilerParams(vmem_limit_bytes=32 * 1024 * 1024),
         cost_estimate=pl.CostEstimate(
             flops=64 * math.prod(out_shape),

time: 54.6 us -> 46.5 us (0.85)
  Pallas kernels: 52.1 us -> 44.2 us
  other arithmetic: 0.86 us -> 0 us
  local copies, waits for them, and re-layouts: 1.39 us -> 2.01 us
    pallas_call x1, Pallas kernels: 22.9 us -> 17.9 us  [local(): pl.pallas_call(functools.partial(products_kernel, row_width, 1.0 / (2 * h...]
    pallas_call x1, Pallas kernels: 29.2 us -> 26.4 us  [local(): pl.pallas_call(functools.partial(coeffs_kernel, rows, width), out_shape=j...]
    unnamed x2 -> x6, local copies, waits for them, and re-layouts: 0.65 us -> 2.01 us
    another operation x2 -> x0, other arithmetic: 0.81 us -> none
    reshape x1 -> x0, local copies, waits for them, and re-layouts: 0.72 us -> none  [local(): live_mask.reshape(1, -1)]
where the time goes in v2:
time: 46.5 us; the launch traced here: 46.3 us
  Pallas kernels  44.2 us (95%)
  local copies, waits for them, and re-layouts  2.01 us (4%)
    pallas_call x1, Pallas kernels, local(): pl.pallas_call(functools.partial(coeffs_kernel, rows, width), out_shape=j...  26.4 us
    pallas_call x1, Pallas kernels, local(): pl.pallas_call(functools.partial(products_kernel, row_width, 1.0 / (2 * h...  17.9 us
    unnamed x6, local copies, waits for them, and re-layouts  2.01 us

profile of v2, /device:TPU:0, one launch (start us, length us, event | category | flops | bytes accessed | tf_op | source)
XLA Modules:
  0.0 46.3 jit_solution(9096685019310567777)
XLA Ops:
  0.0 0.0 copy-start
  0.0 0.7 %copy-done = s32[2560]{0:T(1024)S(1)} copy-done((s32[2560]{0:T(1024)S(1)}, s32[2560]{0:T(1024)}, u32[]{:S(2)}) %copy-start) | copy-done | bytes 10264
  0.7 0.0 copy-start.1
  0.7 0.7 %copy-done.1 = s32[4]{0:T(128)S(1)} copy-done((s32[4]{0:T(128)S(1)}, s32[4]{0:T(128)}, u32[]{:S(2)}) %copy-start.1) | copy-done | bytes 40
  1.4 26.4 %window_coeffs.1.coeffs_ref = bf16[2,32,2560]{2,1,0:T(8,128)(2,1)S(1)} custom-call(s32[4]{0:T(128)S(1)} %copy-done.1, s32[2560]{0:T(1024)S(1)} %copy-done, bf16[4,384,5120]{2,1,0:T(8,128)(2,1)} %records_ref.1), custom_call_target="tpu_custom_call" | custom-call | flops 141557760 | bytes 15728640 | tf_op jit(solution)/shard_map/window_coeffs/pallas_call | solution.py:316
  27.7 0.0 copy-start.2
  27.7 0.6 %copy-done.2 = s32[4]{0:T(128)S(1)} copy-done((s32[4]{0:T(128)S(1)}, s32[4]{0:T(128)}, u32[]{:S(2)}) %copy-start.2) | copy-done | bytes 40
  28.4 17.9 %cross_products.1 = f32[2,2,1280,2560]{3,2,1,0:T(8,128)} custom-call(s32[4]{0:T(128)S(1)} %copy-done.2, bf16[2,32,2560]{2,1,0:T(8,128)(2,1)S(1)} %window_coeffs.1.coeffs_ref), custom_call_target="tpu_custom_call" | custom-call | flops 838860800 | bytes 52428800 | tf_op jit(solution)/shard_map/cross_products/pallas_call | solution.py:350
Async XLA Ops:
  0.0 0.7 %copy-start = (s32[2560]{0:T(1024)S(1)}, s32[2560]{0:T(1024)}, u32[]{:S(2)}) copy-start(s32[2560]{0:T(1024)} %mask_ref.1) | copy-start | bytes 30724
  0.7 0.7 %copy-start.1 = (s32[4]{0:T(128)S(1)}, s32[4]{0:T(128)}, u32[]{:S(2)}) copy-start(s32[4]{0:T(128)} %bins_ref.1) | copy-start | bytes 52
  27.7 0.7 %copy-start.2 = (s32[4]{0:T(128)S(1)}, s32[4]{0:T(128)}, u32[]{:S(2)}) copy-start(s32[4]{0:T(128)} %order_ref.1) | copy-start | bytes 52

commit v3 on v2

--- a/solution.py
+++ b/solution.py
@@ -10,7 +10,6 @@
 
 C = 5120
 S = 3072
-AHEAD = 3
 TILE_ROWS = 256
 SLOTS = 4
 MESH = pl.DeviceIdType.MESH
@@ -72,8 +71,8 @@
 
 def coeffs_kernel(
     rows, width, bins_ref, mask_ref, records_ref, out_ref,
-    rec, table, part, xs, xr, zs, zr, ag,
-    rec_sem, xs_sem, xr_sem, zs_sem, zr_sem, own_sem, gs_sem, gr_sem, fs_sem, fr_sem,
+    rec, bins, mask, table, part, xs, xr, zs, zr, ag,
+    rec_sem, bins_sem, mask_sem, xs_sem, xr_sem, zs_sem, zr_sem, own_sem, gs_sem, gr_sem, fs_sem, fr_sem,
 ):
     r, c, f = lax.axis_index("row"), lax.axis_index("col"), lax.axis_index("freq")
     windows, samples = records_ref.shape[0], records_ref.shape[1]
@@ -132,32 +131,39 @@
     pl.semaphore_signal(barrier, inc=1, device_id={"freq": 1 - f}, device_id_type=MESH)
     pl.semaphore_signal(barrier, inc=1, device_id={"col": 1 - c}, device_id_type=MESH)
 
-    for step in range(AHEAD):
+    bins_copy = pltpu.make_async_copy(bins_ref, bins, bins_sem)
+    bins_copy.start()
+    mask_copy = pltpu.make_async_copy(mask_ref, mask, mask_sem)
+    mask_copy.start()
+    for step in (0, 1, rows):
         load(step).start()
     part[...] = jnp.zeros_like(part)
     row = lax.broadcasted_iota(jnp.int32, (8, samples), 0)
     position = (r * 2 + c) * samples + lax.broadcasted_iota(jnp.int32, (8, samples), 1)
-    bins = jnp.zeros_like(row)
-    for k in range(bins_ref.shape[0]):
-        bins = jnp.where((row >> 1) == k, bins_ref[k], bins)
-    phase = lax.rem(bins * position + (row & 1) * (S // 4), S)
+    bins_copy.wait()
+    bin_rows = jnp.zeros_like(row)
+    for k in range(bins.shape[0]):
+        bin_rows = jnp.where((row >> 1) == k, bins[k], bin_rows)
+    phase = lax.rem(bin_rows * position + (row & 1) * (S // 4), S)
     taper = math.sqrt(16.0 / (3.0 * S)) * (0.5 - 0.5 * cosine(position))
     table[...] = (taper * cosine(phase)).astype(table.dtype)
     pl.semaphore_wait(barrier, 2 * rows)
 
-    @pl.loop(0, rows)
-    def _(step):
-        load(step + AHEAD).start()
+    def send_x(step):
         compute(step)
         xs[step] = part[...].astype(xs.dtype)
         x_copy(step).start()
 
+    send_x(0)
+
     @pl.loop(0, rows - 1)
     def _(step):
-        @pl.when(step + rows + AHEAD < steps)
+        @pl.when(step + 2 < rows)
         def _():
-            load(step + rows + AHEAD).start()
-
+            load(step + 2).start()
+
+        load(rows + step + 1).start()
+        send_x(step + 1)
         compute(step + rows)
         x_copy(step).wait_recv()
         both = part[...] + xr[step].astype(jnp.float32)
@@ -171,8 +177,9 @@
         z_copy(step).wait_recv()
         total = total + zr[step].astype(jnp.float32)[:40]
 
-    mask = mask_ref[pl.ds(pl.multiple_of(r * width, 128), width)].astype(jnp.float32)[None, :]
-    scaling = mask / jnp.sqrt(total[32:36] / S + 1e-06)
+    mask_copy.wait()
+    live = mask[pl.ds(pl.multiple_of(r * width, 128), width)].astype(jnp.float32)[None, :]
+    scaling = live / jnp.sqrt(total[32:36] / S + 1e-06)
     coeffs = jnp.concatenate(
         [total[8 * w : 8 * w + 8] * scaling[w : w + 1] for w in range(windows)], axis=0
     ).astype(jnp.bfloat16)
@@ -310,16 +317,19 @@
     width = block_width // rows
     row_width = C // rows
     smem = pl.BlockSpec(memory_space=pltpu.SMEM)
+    hbm = pl.BlockSpec(memory_space=pltpu.HBM)
     vmem = pl.BlockSpec(memory_space=pltpu.VMEM)
     anywhere = pl.BlockSpec(memory_space=pl.ANY)
     dma = pltpu.SemaphoreType.DMA
     coeffs = pl.pallas_call(
         functools.partial(coeffs_kernel, rows, width),
         out_shape=jax.ShapeDtypeStruct((2, 32, block_width), jnp.bfloat16),
-        in_specs=[smem, vmem, anywhere],
+        in_specs=[hbm, hbm, anywhere],
         out_specs=anywhere,
         scratch_shapes=[
             pltpu.VMEM((2 * rows, half_windows, local_samples, width), jnp.bfloat16),
+            pltpu.SMEM(bin_index.shape, jnp.int32),
+            pltpu.VMEM((block_width,), jnp.int32),
             pltpu.VMEM((8, local_samples), jnp.bfloat16),
             pltpu.VMEM((48, width), jnp.float32),
             pltpu.VMEM((rows, 48, width), jnp.bfloat16),
@@ -328,6 +338,8 @@
             pltpu.VMEM((rows - 1, 48, width), jnp.bfloat16),
             pltpu.VMEM((2, 16, width), jnp.bfloat16),
             dma((2 * rows,)),
+            dma(()),
+            dma(()),
             dma((rows,)),
             dma((rows,)),
             dma((rows - 1,)),

time: 46.5 us -> 48.7 us (1.047)
  Pallas kernels: 44.2 us -> 46.4 us
    pallas_call x1, Pallas kernels: 26.4 us -> 28.6 us  [local(): pl.pallas_call(functools.partial(coeffs_kernel, rows, width), out_shape=j...]
where the time goes in v3:
time: 48.7 us; the launch traced here: 48.5 us
  Pallas kernels  46.4 us (95%)
  local copies, waits for them, and re-layouts  2.01 us (4%)
    pallas_call x1, Pallas kernels, local(): pl.pallas_call(functools.partial(coeffs_kernel, rows, width), out_shape=j...  28.6 us
    pallas_call x1, Pallas kernels, local(): pl.pallas_call(functools.partial(products_kernel, row_width, 1.0 / (2 * h...  17.9 us
    unnamed x6, local copies, waits for them, and re-layouts  2.01 us

profile of v3, /device:TPU:0, one launch (start us, length us, event | category | flops | bytes accessed | tf_op | source)
XLA Modules:
  0.0 48.5 jit_solution(4019371358571405238)
XLA Ops:
  0.0 0.0 copy-start
  0.0 0.7 %copy-done = s32[2560]{0:T(1024)S(1)} copy-done((s32[2560]{0:T(1024)S(1)}, s32[2560]{0:T(1024)}, u32[]{:S(2)}) %copy-start) | copy-done | bytes 10264
  0.7 0.0 copy-start.1
  0.7 0.7 %copy-done.1 = s32[4]{0:T(128)S(1)} copy-done((s32[4]{0:T(128)S(1)}, s32[4]{0:T(128)}, u32[]{:S(2)}) %copy-start.1) | copy-done | bytes 40
  1.4 28.6 %window_coeffs.1.coeffs_ref = bf16[2,32,2560]{2,1,0:T(8,128)(2,1)S(1)} custom-call(s32[4]{0:T(128)S(1)} %copy-done.1, s32[2560]{0:T(1024)S(1)} %copy-done, bf16[4,384,5120]{2,1,0:T(8,128)(2,1)} %records_ref.1), custom_call_target="tpu_custom_call" | custom-call | flops 141557760 | bytes 15728640 | tf_op jit(solution)/shard_map/window_coeffs/pallas_call | solution.py:324
  30.0 0.0 copy-start.2
  30.0 0.6 %copy-done.2 = s32[4]{0:T(128)S(1)} copy-done((s32[4]{0:T(128)S(1)}, s32[4]{0:T(128)}, u32[]{:S(2)}) %copy-start.2) | copy-done | bytes 40
  30.6 17.9 %cross_products.1 = f32[2,2,1280,2560]{3,2,1,0:T(8,128)} custom-call(s32[4]{0:T(128)S(1)} %copy-done.2, bf16[2,32,2560]{2,1,0:T(8,128)(2,1)S(1)} %window_coeffs.1.coeffs_ref), custom_call_target="tpu_custom_call" | custom-call | flops 838860800 | bytes 52428800 | tf_op jit(solution)/shard_map/cross_products/pallas_call | solution.py:362
Async XLA Ops:
  0.0 0.7 %copy-start = (s32[2560]{0:T(1024)S(1)}, s32[2560]{0:T(1024)}, u32[]{:S(2)}) copy-start(s32[2560]{0:T(1024)} %mask_ref.1) | copy-start | bytes 30724
  0.7 0.7 %copy-start.1 = (s32[4]{0:T(128)S(1)}, s32[4]{0:T(128)}, u32[]{:S(2)}) copy-start(s32[4]{0:T(128)} %bins_ref.1) | copy-start | bytes 52
  30.0 0.7 %copy-start.2 = (s32[4]{0:T(128)S(1)}, s32[4]{0:T(128)}, u32[]{:S(2)}) copy-start(s32[4]{0:T(128)} %order_ref.1) | copy-start | bytes 52

commit v4 on v3

--- a/solution.py
+++ b/solution.py
@@ -10,6 +10,7 @@
 
 C = 5120
 S = 3072
+AHEAD = 3
 TILE_ROWS = 256
 SLOTS = 4
 MESH = pl.DeviceIdType.MESH
@@ -135,7 +136,7 @@
     bins_copy.start()
     mask_copy = pltpu.make_async_copy(mask_ref, mask, mask_sem)
     mask_copy.start()
-    for step in (0, 1, rows):
+    for step in range(AHEAD):
         load(step).start()
     part[...] = jnp.zeros_like(part)
     row = lax.broadcasted_iota(jnp.int32, (8, samples), 0)
@@ -149,21 +150,19 @@
     table[...] = (taper * cosine(phase)).astype(table.dtype)
     pl.semaphore_wait(barrier, 2 * rows)
 
-    def send_x(step):
+    @pl.loop(0, rows)
+    def _(step):
+        load(step + AHEAD).start()
         compute(step)
         xs[step] = part[...].astype(xs.dtype)
         x_copy(step).start()
 
-    send_x(0)
-
     @pl.loop(0, rows - 1)
     def _(step):
-        @pl.when(step + 2 < rows)
+        @pl.when(step + rows + AHEAD < steps)
         def _():
-            load(step + 2).start()
-
-        load(rows + step + 1).start()
-        send_x(step + 1)
+            load(step + rows + AHEAD).start()
+
         compute(step + rows)
         x_copy(step).wait_recv()
         both = part[...] + xr[step].astype(jnp.float32)
@@ -351,7 +350,7 @@
             dma((rows, 2)),
         ],
         compiler_params=pltpu.CompilerParams(
-            collective_id=0, has_side_effects=True, vmem_limit_bytes=40 * 1024 * 1024
+            collective_id=0, has_side_effects=True, vmem_limit_bytes=65152 * 1024
         ),
         cost_estimate=pl.CostEstimate(
             flops=18 * records.size, bytes_accessed=2 * records.size, transcendentals=0
@@ -368,7 +367,7 @@
             pltpu.VMEM((SLOTS, TILE_ROWS, block_width), jnp.float32),
             dma((SLOTS,)),
         ],
-        compiler_params=pltpu.CompilerParams(vmem_limit_bytes=32 * 1024 * 1024),
+        compiler_params=pltpu.CompilerParams(vmem_limit_bytes=65152 * 1024),
         cost_estimate=pl.CostEstimate(
             flops=64 * math.prod(out_shape),
             bytes_accessed=4 * math.prod(out_shape),

time: 48.7 us -> 44.7 us (0.918)
  local copies, waits for them, and re-layouts: 2.01 us -> 0 us
  Pallas kernels: 46.4 us -> 44.5 us
    pallas_call x1, Pallas kernels: 28.6 us -> 26.2 us  [local(): pl.pallas_call(functools.partial(coeffs_kernel, rows, width), out_shape=j...]
    unnamed x6 -> x0, local copies, waits for them, and re-layouts: 2.01 us -> none
where the time goes in v4:
time: 44.7 us; the launch traced here: 44.5 us
  Pallas kernels  44.5 us (100%)
    pallas_call x1, Pallas kernels, local(): pl.pallas_call(functools.partial(coeffs_kernel, rows, width), out_shape=j...  26.2 us
    pallas_call x1, Pallas kernels, local(): pl.pallas_call(functools.partial(products_kernel, row_width, 1.0 / (2 * h...  18.3 us

profile of v4, /device:TPU:0, one launch (start us, length us, event | category | flops | bytes accessed | tf_op | source)
XLA Modules:
  0.0 44.5 jit_solution(9794921704416327736)
XLA Ops:
  0.0 26.2 %window_coeffs.1.coeffs_ref = bf16[2,32,2560]{2,1,0:T(8,128)(2,1)} custom-call(s32[4]{0:T(128)} %bins_ref.1, s32[2560]{0:T(1024)} %mask_ref.1, bf16[4,384,5120]{2,1,0:T(8,128)(2,1)} %records_ref.1), custom_call_target="tpu_custom_call" | custom-call | flops 141557760 | bytes 15728640 | tf_op jit(solution)/shard_map/window_coeffs/pallas_call | solution.py:323
  26.2 18.3 %cross_products.1 = f32[2,2,1280,2560]{3,2,1,0:T(8,128)} custom-call(s32[4]{0:T(128)} %order_ref.1, bf16[2,32,2560]{2,1,0:T(8,128)(2,1)} %window_coeffs.1.coeffs_ref), custom_call_target="tpu_custom_call" | custom-call | flops 838860800 | bytes 52428800 | tf_op jit(solution)/shard_map/cross_products/pallas_call | solution.py:361
